TPU v7x, 256 devices: a whole 4x4x8 slice. The times are simulated.
256 devices in a mesh: band: 32 (over z, x), gvec: 8 (over y, core).
Axes of the slice: x: 4, y: 4, z: 8, core: 2. Of those that a mesh axis runs over, the one named last changes fastest.
Arguments:
- pairs: bfloat16 [32, 8, 512, 640], P(None, 'gvec', 'band'), may hold values from -0.59765625 to 0.59765625
- cond_energy: float32 [512], replicated, may hold values from 0.5 to 12
- val_energy: float32 [32, 8], replicated, may hold values from -12 to -2
- band_counts: int32 [32], replicated, may hold values from 1 to 16, as said below
- slab: int32 [1], replicated, may hold values from 0 to 31
Outputs:
- chi_zero: float32 [20480, 20480], P('gvec', 'band')
Inputs may be any that keep to these rules, and one draw needn't show every extreme that they name: `band_counts`: every owner has at least one occupied slot, and in every draw some owner has all 16 slots occupied.
All inputs are finite; a program needn't handle non-finite values.
Results may differ from a plain program's by a relative error of at most 0.0028.
Values may be sent and summed in bfloat16 or wider, within the bound.
No kernel may reach another device: no remote copies, remote signals or barrier semaphores. Data moves between devices by JAX's collectives and lax.ppermute only.
A program may use at most 128 MiB of HBM per device.

v0:
```python
import jax
import jax.numpy as jnp
from jax import lax
from jax.sharding import PartitionSpec as P


def on_device(pairs, cond_energy, val_energy, band_counts, slab):
    n_band = lax.axis_size("band")
    n_gvec = lax.axis_size("gvec")
    ratio = n_band // n_gvec
    local_v = pairs.shape[1]
    slot_count = pairs.shape[2]
    col_width = pairs.shape[3]
    energies = lax.dynamic_index_in_dim(val_energy, slab[0], 0, keepdims=False)
    slots = jnp.arange(slot_count, dtype=jnp.int32)
    live = (slots[None, :] < band_counts[:, None]).reshape(-1)
    weight = jnp.where(
        live[None, :], 2.0 / (energies[:, None] - cond_energy[None, :]), jnp.float32(0.0)
    )
    blocked = pairs.reshape(n_gvec, ratio, local_v, slot_count, col_width)
    by_block = lax.all_to_all(blocked, "gvec", split_axis=0, concat_axis=2, tiled=True)
    rows_all = lax.all_gather(by_block, "band", axis=3, tiled=True)[0]
    by_column = lax.all_to_all(pairs, "band", split_axis=0, concat_axis=2, tiled=True)
    cols_all = lax.all_gather(by_column, "gvec", axis=1, tiled=True)[0]
    scaled = (weight[:, :, None] * cols_all.astype(jnp.float32)).astype(jnp.bfloat16)
    result = lax.dot_general(
        rows_all, scaled, (((1, 2), (0, 1)), ((), ())), preferred_element_type=jnp.float32
    )
    return result.reshape(ratio * col_width, col_width)


def solution(mesh):
    in_specs = (P(None, "gvec", "band", None), P(), P(), P(), P())
    out_specs = P("gvec", "band")
    return jax.shard_map(
        on_device, mesh=mesh, in_specs=in_specs, out_specs=out_specs, check_vma=False
    )
```

profile of v0, /device:TPU:1, one launch (start us, length us, event | category | flops | bytes accessed | tf_op | source)
XLA Modules:
  0.0 263.4 jit_solution(6837848196494836438)
XLA Ops:
  6.5 0.0 copy-start
  6.5 0.0 all-gather.6.cloned.1.call-start
  6.5 17.7 %all_to_all.30 = bf16[8,4,1,16,640]{4,3,2,1,0:T(8,128)(2,1)S(1)} all-to-all(bf16[8,4,1,16,640]{4,3,2,1,0:T(8,128)(2,1)} %bitcast.24), channel_id=1, replica_groups=mesh['band'=32,'gvec'=8] {'gvec'}, dimensions={0} | all-to-all | bytes 1310720 | tf_op jit(solution)/shard_map/all_to_all | solution.py:21
  24.3 1.2 copy.8
  25.5 0.0 all-gather.6.cloned.1.call-update
  25.5 0.0 all-gather.4.cloned.1.call-start
  25.6 32.6 %all_to_all.31 = bf16[32,1,16,640]{3,2,1,0:T(8,128)(2,1)} all-to-all(bf16[32,1,16,640]{3,2,1,0:T(8,128)(2,1)} %param.5), channel_id=1, replica_groups=mesh['band'=32,'gvec'=8] {'band'}, dimensions={0} | all-to-all | bytes 1310720 | tf_op jit(solution)/shard_map/all_to_all | solution.py:23
  58.2 0.0 all-gather.4.cloned.1.call-update
  58.8 0.7 iota_compare_fusion
  59.6 0.1 lt.27
  59.7 0.0 copy-done
  59.7 0.2 dynamic-slice_reduce_fusion
  59.8 0.8 divide_select_fusion
  60.6 133.8 %all-gather.6.cloned.1.call-done = bf16[1,4,8,1,512,640]{5,2,3,1,0,4:T(8,128)(2,1)} async-done(((bf16[1,4,8,1,16,640]{5,2,3,1,0,4:T(8,128)(2,1)}), bf16[1,4,8,1,512,640]{5,2,3,1,0,4:T(8,128)(2,1)}) %all-gather.6.cloned.1.call-update) | async-done | bytes 20971536 | tf_op jit(solution)/shard_map/all_gather | solution.py:22
  194.4 30.2 %copy.9 = bf16[1,4,8,1,512,640]{4,5,2,1,3,0:T(8,128)(2,1)} copy(bf16[1,4,8,1,512,640]{5,2,3,1,0,4:T(8,128)(2,1)} %all-gather.6.cloned.1.call-done) | data formatting | bytes 41943040 | tf_op jit(solution)/shard_map/all_gather | solution.py:22
  224.6 8.6 %all-gather.4.cloned.1.call-done = bf16[1,8,512,640]{3,2,0,1:T(8,128)(2,1)} async-done(((bf16[1,1,512,640]{3,2,0,1:T(8,128)(2,1)}), bf16[1,8,512,640]{3,2,0,1:T(8,128)(2,1)}) %all-gather.4.cloned.1.call-update) | async-done | bytes 5242896 | tf_op jit(solution)/shard_map/all_gather | solution.py:24
  233.3 23.3 %fusion = f32[640,4,640,1]{0,2,3,1:T(8,128)} fusion(bf16[1,4,8,1,512,640]{4,5,2,1,3,0:T(8,128)(2,1)} %copy.9, bf16[1,8,512,640]{3,2,0,1:T(8,128)(2,1)} %all-gather.4.cloned.1.call-done, f32[8,512]{1,0:T(8,128)S(1)} %divide_select_fusion), kind=kOutput, calls=%fused_computation | convolution fusion | flops 13429637120 | bytes 32784384 | tf_op jit(solution)/shard_map/dot_general | solution.py:26
Async XLA Ops:
  6.5 53.1 %copy-start = (f32[32,8]{0,1:T(8,128)S(1)}, f32[32,8]{0,1:T(8,128)}, u32[]{:S(2)}) copy-start(f32[32,8]{0,1:T(8,128)} %param.7) | copy-start | bytes 3076
  6.5 187.9 %all-gather.6.cloned.1.call-start = ((), (), s32[]{:S(2)}) async-start(), calls=%async_computation.3 | async-start | bytes 21626880 | tf_op jit(solution)/shard_map/all_gather | solution.py:22
  25.5 207.7 %all-gather.4.cloned.1.call-start = ((), (), s32[]{:S(2)}) async-start(), calls=%async_computation.2 | async-start | bytes 5898240 | tf_op jit(solution)/shard_map/all_gather | solution.py:24
Sparse Core Ops, SparseCore 0:
  25.6 168.7 all-gather.5
  196.3 36.9 all-gather.3
where the time goes:
time: 264 us; the launch traced here: 263 us
  waiting for transfers between devices  142 us (54%)
  blocking collectives  50.3 us (19%)
  local copies, waits for them, and re-layouts  31.7 us (12%)
  matrix products  23.3 us (9%)
  between operations  14.1 us (5%)
    all_gather x1, waiting for transfers between devices, on_device(): rows_all = lax.all_gather(by_block, 'band', axis=3, tiled=True)[0]  134 us
    all_to_all x1, blocking collectives, on_device(): lax.all_to_all(pairs, 'band', split_axis=0, concat_axis=2, tiled=True)  32.6 us
    all_gather x1, local copies, waits for them, and re-layouts, on_device(): rows_all = lax.all_gather(by_block, 'band', axis=3, tiled=True)[0]  30.2 us
    dot_general x1, matrix products, on_device(): lax.dot_general(rows_all, scaled, (((1, 2), (0, 1)), ((), ())), preferred...  23.3 us
    all_to_all x1, blocking collectives, on_device(): lax.all_to_all(blocked, 'gvec', split_axis=0, concat_axis=2, tiled=True)  17.7 us
    all_gather x1, waiting for transfers between devices, on_device(): cols_all = lax.all_gather(by_column, 'gvec', axis=1, tiled=True)[0]  8.62 us
  transfers between devices with their start and end apart: 2, of which 2 were waited for; matrix products, arithmetic and copies ran while one was open for 12% of the time, Pallas kernels for 0%

commit v1 on v0

--- a/solution.py
+++ b/solution.py
@@ -20,7 +20,10 @@
     blocked = pairs.reshape(n_gvec, ratio, local_v, slot_count, col_width)
     by_block = lax.all_to_all(blocked, "gvec", split_axis=0, concat_axis=2, tiled=True)
     rows_all = lax.all_gather(by_block, "band", axis=3, tiled=True)[0]
-    by_column = lax.all_to_all(pairs, "band", split_axis=0, concat_axis=2, tiled=True)
+    by_column = jnp.concatenate(
+        lax.all_to_all(jnp.stack(jnp.split(pairs, lax.axis_size("band"), axis=0)), "band", 0, 0),
+        axis=2,
+    )
     cols_all = lax.all_gather(by_column, "gvec", axis=1, tiled=True)[0]
     scaled = (weight[:, :, None] * cols_all.astype(jnp.float32)).astype(jnp.bfloat16)
     result = lax.dot_general(

time: 264 us -> 271 us (1.027)
  local copies, waits for them, and re-layouts: 31.7 us -> 55.2 us
  waiting for transfers between devices: 142 us -> 121 us
    unnamed x2 -> x33, local copies, waits for them, and re-layouts: 0.01 us -> 22.8 us
    all_gather x1, waiting for transfers between devices: 134 us -> 113 us  [on_device(): rows_all = lax.all_gather(by_block, 'band', axis=3, tiled=True)[0]]
  transfers between devices with their start and end apart: 2 -> 2, of which waited for: 2 -> 2; matrix products, arithmetic and copies ran while one was open for 12% -> 21% of each run, Pallas kernels for 0% -> 0%
where the time goes in v1:
time: 271 us; the launch traced here: 269 us
  waiting for transfers between devices  121 us (45%)
  local copies, waits for them, and re-layouts  55.2 us (20%)
  blocking collectives  52.9 us (20%)
  matrix products  23.3 us (9%)
  between operations  14.1 us (5%)
    all_gather x1, waiting for transfers between devices, on_device(): rows_all = lax.all_gather(by_block, 'band', axis=3, tiled=True)[0]  113 us
    all_to_all x1, blocking collectives, on_device(): lax.all_to_all(jnp.stack(jnp.split(pairs, lax.axis_size('band'), axis=0))...  35.2 us
    all_gather x1, local copies, waits for them, and re-layouts, on_device(): rows_all = lax.all_gather(by_block, 'band', axis=3, tiled=True)[0]  30.2 us
    dot_general x1, matrix products, on_device(): lax.dot_general(rows_all, scaled, (((1, 2), (0, 1)), ((), ())), preferred...  23.3 us
    unnamed x33, local copies, waits for them, and re-layouts  22.8 us
    all_to_all x1, blocking collectives, on_device(): lax.all_to_all(blocked, 'gvec', split_axis=0, concat_axis=2, tiled=True)  17.7 us
    all_gather x1, waiting for transfers between devices, on_device(): cols_all = lax.all_gather(by_column, 'gvec', axis=1, tiled=True)[0]  8.62 us
  transfers between devices with their start and end apart: 2, of which 2 were waited for; matrix products, arithmetic and copies ran while one was open for 21% of the time, Pallas kernels for 0%

profile of v1, /device:TPU:1, one launch (start us, length us, event | category | flops | bytes accessed | tf_op | source)
XLA Modules:
  0.0 268.5 jit_solution(13973692429775609040)
XLA Ops:
  6.5 0.0 copy-start
  6.5 0.0 all-gather.6.cloned.1.call-start
  6.5 17.7 %all_to_all.23 = bf16[8,4,1,16,640]{4,3,2,1,0:T(8,128)(2,1)S(1)} all-to-all(bf16[8,4,1,16,640]{4,3,2,1,0:T(8,128)(2,1)} %bitcast.90), channel_id=1, replica_groups=mesh['band'=32,'gvec'=8] {'gvec'}, dimensions={0} | all-to-all | bytes 1310720 | tf_op jit(solution)/shard_map/all_to_all | solution.py:21
  24.3 1.2 copy.8
  25.5 0.0 all-gather.6.cloned.1.call-update
  25.5 0.0 all-gather.4.cloned.1.call-start
  25.6 0.7 constant_dynamic-update-slice_fusion.31
  26.3 0.7 constant_dynamic-update-slice_fusion.30
  27.0 0.7 constant_dynamic-update-slice_fusion.29
  27.8 0.7 constant_dynamic-update-slice_fusion.28
  28.5 0.7 constant_dynamic-update-slice_fusion.27
  29.2 0.7 constant_dynamic-update-slice_fusion.26
  30.0 0.7 constant_dynamic-update-slice_fusion.25
  30.7 0.7 constant_dynamic-update-slice_fusion.24
  31.5 0.7 constant_dynamic-update-slice_fusion.23
  32.2 0.7 constant_dynamic-update-slice_fusion.22
  32.9 0.7 constant_dynamic-update-slice_fusion.21
  33.7 0.7 constant_dynamic-update-slice_fusion.20
  34.4 0.7 constant_dynamic-update-slice_fusion.19
  35.1 0.7 constant_dynamic-update-slice_fusion.18
  35.9 0.7 constant_dynamic-update-slice_fusion.17
  36.6 0.7 constant_dynamic-update-slice_fusion.16
  37.3 0.7 constant_dynamic-update-slice_fusion.15
  38.1 0.7 constant_dynamic-update-slice_fusion.14
  38.8 0.7 constant_dynamic-update-slice_fusion.13
  39.6 0.7 constant_dynamic-update-slice_fusion.12
  40.3 0.7 constant_dynamic-update-slice_fusion.11
  41.0 0.7 constant_dynamic-update-slice_fusion.10
  41.8 0.7 constant_dynamic-update-slice_fusion.9
  42.5 0.7 constant_dynamic-update-slice_fusion.8
  43.2 0.7 constant_dynamic-update-slice_fusion.7
  44.0 0.7 constant_dynamic-update-slice_fusion.6
  44.7 0.7 constant_dynamic-update-slice_fusion.5
  45.4 0.7 constant_dynamic-update-slice_fusion.4
  46.2 0.7 constant_dynamic-update-slice_fusion.3
  46.9 0.7 constant_dynamic-update-slice_fusion.2
  47.6 0.7 constant_dynamic-update-slice_fusion.1
  48.4 0.7 constant_dynamic-update-slice_fusion
  49.1 35.2 %all_to_all.24 = bf16[32,1,1,16,640]{4,3,2,1,0:T(8,128)(2,1)} all-to-all(bf16[32,1,1,16,640]{4,3,2,1,0:T(8,128)(2,1)S(1)} %constant_dynamic-update-slice_fusion), channel_id=1, replica_groups=mesh['band'=32,'gvec'=8] {'band'}, dimensions={0} | all-to-all | bytes 1310720 | tf_op jit(solution)/shard_map/all_to_all | solution.py:24
  84.3 0.0 all-gather.4.cloned.1.call-update
  85.0 0.7 iota_compare_fusion
  85.7 0.1 lt.27
  85.8 0.2 dynamic-slice_reduce_fusion
  86.0 0.8 divide_select_fusion
  86.8 112.8 %all-gather.6.cloned.1.call-done = bf16[1,4,8,1,512,640]{5,2,3,1,0,4:T(8,128)(2,1)} async-done(((bf16[1,4,8,1,16,640]{5,2,3,1,0,4:T(8,128)(2,1)}), bf16[1,4,8,1,512,640]{5,2,3,1,0,4:T(8,128)(2,1)}) %all-gather.6.cloned.1.call-update) | async-done | bytes 20971536 | tf_op jit(solution)/shard_map/all_gather | solution.py:22
  199.5 30.2 %copy.9 = bf16[1,4,8,1,512,640]{4,5,2,1,3,0:T(8,128)(2,1)} copy(bf16[1,4,8,1,512,640]{5,2,3,1,0,4:T(8,128)(2,1)} %all-gather.6.cloned.1.call-done) | data formatting | bytes 41943040 | tf_op jit(solution)/shard_map/all_gather | solution.py:22
  229.8 8.6 %all-gather.4.cloned.1.call-done = bf16[1,8,512,640]{3,2,0,1:T(8,128)(2,1)} async-done(((bf16[1,1,512,640]{3,2,0,1:T(8,128)(2,1)}), bf16[1,8,512,640]{3,2,0,1:T(8,128)(2,1)}) %all-gather.4.cloned.1.call-update) | async-done | bytes 5242896 | tf_op jit(solution)/shard_map/all_gather | solution.py:27
  238.4 23.3 %fusion = f32[640,4,640,1]{0,2,3,1:T(8,128)} fusion(bf16[1,4,8,1,512,640]{4,5,2,1,3,0:T(8,128)(2,1)} %copy.9, bf16[1,8,512,640]{3,2,0,1:T(8,128)(2,1)} %all-gather.4.cloned.1.call-done, f32[8,512]{1,0:T(8,128)S(1)} %divide_select_fusion), kind=kOutput, calls=%fused_computation | convolution fusion | flops 13429637120 | bytes 32784384 | tf_op jit(solution)/shard_map/dot_general | solution.py:29
  (1 shorter events, 0.0 us)
Async XLA Ops:
  6.5 79.3 %copy-start = (f32[32,8]{0,1:T(8,128)S(1)}, f32[32,8]{0,1:T(8,128)}, u32[]{:S(2)}) copy-start(f32[32,8]{0,1:T(8,128)} %param.7) | copy-start | bytes 3076
  6.5 193.0 %all-gather.6.cloned.1.call-start = ((), (), s32[]{:S(2)}) async-start(), calls=%async_computation.3 | async-start | bytes 21626880 | tf_op jit(solution)/shard_map/all_gather | solution.py:22
  25.5 212.9 %all-gather.4.cloned.1.call-start = ((), (), s32[]{:S(2)}) async-start(), calls=%async_computation.2 | async-start | bytes 5898240 | tf_op jit(solution)/shard_map/all_gather | solution.py:27
Sparse Core Ops, SparseCore 0:
  25.6 173.8 all-gather.5
  201.4 36.9 all-gather.3
